TPU v7x, 32 devices: a whole 2x2x4 slice. The times are simulated.
32 devices in a mesh: dom: 8 (over y, x, core), blk: 4 (over z).
Axes of the slice: x: 2, y: 2, z: 4, core: 2. Of those that a mesh axis runs over, the one named last changes fastest.
Arguments:
- features: bfloat16 [32768, 128], P(('dom', 'blk')), may hold values from -6 to 6
- tile_vals: bfloat16 [2304, 128, 128], P(('dom', 'blk')), may hold values from -0.25 to 0.25
- tile_rows: int32 [32, 72], P(('dom', 'blk')), may hold values from 0 to 7
- tile_cols: int32 [32, 72], P(('dom', 'blk')), may hold values from 0 to 7
- tile_count: int32 [32, 4], P(('dom', 'blk')), may hold values from 1 to 18, as said below
- cut_weights: bfloat16 [32768, 384], P(('dom', 'blk')), may hold values from -0.4375 to 0.4375
- send_idx: int32 [32, 384], P(('dom', 'blk')), may hold values from 0 to 1023
- send_count: int32 [32, 8], P(('dom', 'blk')), may hold values from 0 to 48, as said below
- weight: bfloat16 [128, 256], replicated, may hold values from -0.5 to 0.5
- bias: float32 [256], replicated, may hold values from -3 to 3
- cotangent: bfloat16 [32768, 256], P(('dom', 'blk')), may hold values from -6 to 6
Outputs:
- out_y: bfloat16 [32768, 256], P(('dom', 'blk'))
- grad_x: bfloat16 [32768, 128], P(('dom', 'blk'))
- grad_w: float32 [128, 256], replicated
- grad_b: float32 [256], replicated
Inputs may be any that keep to these rules, and one draw needn't show every extreme that they name: `tile_count`: every device has a source position with exactly 18 live slots; devices differ strongly in their counts. `send_count`: zero toward a device's own group; at each index along blk some group receives exactly 48 rows from every other group.
All inputs are finite; a program needn't handle non-finite values.
Results may differ from a plain program's by a relative error of at most 0.018.
Values may be sent and summed in bfloat16 or wider, within the bound.
A program may use at most 128 MiB of HBM per device.

v0:
```python
import math

import jax
import jax.numpy as jnp
from jax import lax
from jax.sharding import PartitionSpec as P


def pad_piece(piece, tile_side):
    padding = jnp.zeros((tile_side, piece.shape[1]), piece.dtype)
    return jnp.concatenate([padding, piece, padding], axis=0)


def pick_blocks(padded, piece_rows, first_rows, tile_side):
    places = jnp.clip(first_rows + tile_side, 0, piece_rows + tile_side)
    picked = jax.vmap(lambda where_at: lax.dynamic_slice_in_dim(padded, where_at, tile_side, 0))(
        places
    )
    inside = (first_rows > -tile_side) & (first_rows < piece_rows)
    return (picked, inside)


def accumulate(running, tiles_here, picked, target, live, flipped):
    row_blocks = running.shape[0]
    selector = (
        (target[:, None] == jnp.arange(row_blocks, dtype=jnp.int32)[None, :]) & live[:, None]
    ).astype(tiles_here.dtype)
    pattern = "tr,tji,tjf->rif" if flipped else "tr,tij,tjf->rif"
    return running + jnp.einsum(
        pattern, selector, tiles_here, picked, preferred_element_type=jnp.float32
    )


def shards(
    features,
    tile_vals,
    tile_rows,
    tile_cols,
    tile_count,
    cut_weights,
    send_idx,
    send_count,
    weight,
    bias,
    cotangent,
):
    rows_dev, feature_width = features.shape
    tile_side = tile_vals.shape[1]
    blk_size = lax.axis_size("blk")
    dom_size = lax.axis_size("dom")
    position = lax.axis_index("blk")
    row_blocks = rows_dev // tile_side
    slot_count = tile_vals.shape[0] // blk_size
    send_most = send_idx.shape[1] // dom_size
    tiles = tile_vals.reshape(blk_size, slot_count, tile_side, tile_side)
    row_ids = tile_rows.reshape(blk_size, slot_count)
    col_ids = tile_cols.reshape(blk_size, slot_count)
    counts = tile_count.reshape(blk_size)
    slot_ids = jnp.arange(slot_count, dtype=jnp.int32)
    live_all = slot_ids[None, :] < counts[:, None]
    sent_rows = send_idx.reshape(dom_size * send_most)
    sent_live = (
        jnp.arange(send_most, dtype=jnp.int32)[None, :] < send_count.reshape(dom_size)[:, None]
    )
    outgoing = jnp.take(features, sent_rows, axis=0).reshape(dom_size, send_most, feature_width)
    outgoing = jnp.where(sent_live[:, :, None], outgoing, jnp.zeros_like(outgoing))
    received = lax.all_to_all(outgoing, "dom", split_axis=0, concat_axis=0, tiled=True)
    cut_part = jnp.dot(
        cut_weights,
        received.reshape(dom_size * send_most, feature_width),
        preferred_element_type=jnp.float32,
    )
    empty = jnp.zeros((row_blocks, tile_side, feature_width), jnp.float32)
    piece = lax.all_gather(features, "blk", axis=0, tiled=True)
    start = jnp.int32(0)
    piece_rows = piece.shape[0]
    padded = pad_piece(piece, tile_side)

    def one_step(source_step, partial_value):
        source = (position - source_step) % blk_size
        lowest = source * rows_dev
        touches = (lowest < start + piece_rows) & (lowest + rows_dev > start)

        def work(inner):
            firsts = lowest + col_ids[source_step] * tile_side
            picked, inside = pick_blocks(padded, piece_rows, firsts, tile_side)
            return accumulate(
                inner,
                tiles[source_step],
                picked,
                row_ids[source_step],
                inside & live_all[source_step],
                False,
            )

        return lax.cond(touches, work, lambda inner: inner, partial_value)

    intra = lax.fori_loop(0, blk_size, one_step, empty).reshape(rows_dev, feature_width)
    aggregated = (intra + cut_part).astype(jnp.bfloat16)
    pre = jnp.dot(aggregated, weight, preferred_element_type=jnp.float32) + bias
    sigmoid_pre = jax.nn.sigmoid(pre)
    out_y = (pre * sigmoid_pre).astype(jnp.bfloat16)
    dpre = (cotangent.astype(jnp.float32) * sigmoid_pre * (1.0 + pre * (1.0 - sigmoid_pre))).astype(
        jnp.bfloat16
    )
    weight_term = lax.dot_general(
        aggregated, dpre, (((0,), (0,)), ((), ())), preferred_element_type=jnp.float32
    )
    bias_term = jnp.sum(dpre.astype(jnp.float32), axis=0)
    dz_rows = lax.dot_general(
        dpre, weight, (((1,), (1,)), ((), ())), preferred_element_type=jnp.float32
    ).astype(jnp.bfloat16)
    cut_back = lax.dot_general(
        cut_weights, dz_rows, (((0,), (0,)), ((), ())), preferred_element_type=jnp.float32
    ).astype(jnp.bfloat16)
    returned = lax.all_to_all(
        cut_back.reshape(dom_size, send_most, feature_width),
        "dom",
        split_axis=0,
        concat_axis=0,
        tiled=True,
    )
    returned = jnp.where(sent_live[:, :, None], returned.astype(jnp.float32), 0.0)
    cut_grad = (
        jnp.zeros((rows_dev, feature_width), jnp.float32)
        .at[sent_rows]
        .add(returned.reshape(dom_size * send_most, feature_width))
    )
    dz_blocks = dz_rows.reshape(row_blocks, tile_side, feature_width)
    row_total = rows_dev * lax.axis_size("blk")

    def one_panel(panel_idx):
        source_step = (position - panel_idx) % blk_size
        picked = jnp.take(dz_blocks, row_ids[source_step], axis=0)
        return accumulate(
            empty, tiles[source_step], picked, col_ids[source_step], live_all[source_step], True
        )

    panel_ids = jnp.arange(row_total // rows_dev, dtype=jnp.int32)
    intra_grad = lax.psum_scatter(
        lax.map(one_panel, panel_ids).reshape(row_total, feature_width),
        "blk",
        scatter_dimension=0,
        tiled=True,
    )
    weight_sum, bias_sum = lax.psum((weight_term, bias_term), ("dom", "blk"))
    scale = 1.0 / math.sqrt(dom_size * blk_size * rows_dev)
    grad_x = (intra_grad + cut_grad).astype(jnp.bfloat16)
    return (out_y, grad_x, weight_sum * scale, bias_sum * scale)


def solution(mesh):
    in_specs = (
        P(("dom", "blk"), None),
        P(("dom", "blk"), None, None),
        P(("dom", "blk"), None),
        P(("dom", "blk"), None),
        P(("dom", "blk"), None),
        P(("dom", "blk"), None),
        P(("dom", "blk"), None),
        P(("dom", "blk"), None),
        P(),
        P(),
        P(("dom", "blk"), None),
    )
    out_specs = (P(("dom", "blk"), None), P(("dom", "blk"), None), P(), P())
    return jax.shard_map(shards, mesh=mesh, in_specs=in_specs, out_specs=out_specs, check_vma=False)
```

profile of v0, /device:TPU:0, one launch (start us, length us, event | category | flops | bytes accessed | tf_op | source)
XLA Modules:
  0.0 325.4 jit_solution(1108997307019440022)
XLA Ops:
  7.2 0.7 all-gather.2.cloned.1.call-update
  7.9 0.7 reduce.2
  8.7 0.7 fusion.45
  9.4 2.2 gather_fusion.1
  11.6 0.7 iota_compare_fusion.2
  12.3 0.8 select_select_fusion
  13.1 5.2 %all-to-all-start = ((bf16[8,48,128]{2,1,0:T(8,128)(2,1)}), bf16[8,48,128]{2,1,0:T(8,128)(2,1)S(1)}, u32[]{:S(2)}, u32[]{:S(2)}) async-start(bf16[8,48,128]{2,1,0:T(8,128)(2,1)} %select_select_fusion), calls=%async_computation | async-start | bytes 196608 | tf_op jit(solution)/shard_map/all_to_all | solution.py:67
  18.9 1.3 reduce.10
  20.2 1.3 reduce.9
  21.7 0.7 iota_compare_fusion.3
  22.4 17.8 %all-gather.2.cloned.1.call-done = bf16[4096,128]{1,0:T(8,128)(2,1)} async-done(((bf16[1024,128]{1,0:T(8,128)(2,1)}), bf16[4096,128]{1,0:T(8,128)(2,1)}) %all-gather.2.cloned.1.call-update) | async-done | bytes 1048592 | tf_op jit(solution)/shard_map/all_gather | solution.py:74
  40.3 1.3 pad_maximum_fusion
  41.6 99.8 %while.34 = (s32[]{:T(128)}, f32[8,128,128]{1,0,2:T(8,128)S(1)}, s32[]{:T(128)}, s32[4,18]{1,0:T(4,128)S(1)}, bf16[4352,128]{1,0:T(8,128)(2,1)S(1)}, /*index=5*/...) while((s32[]{:T(128)}, f32[8,128,128]{1,0,2:T(8,128)S(1)}, ...), condition=%wide.region_3.4_spmd.clone, body=%wide.region_0.3_spmd.clone.sunk | while | flops 80347744 | bytes 3475381 | solution.py:98
  41.7 24.9 %conditional.3 = (f32[8,128,128]{1,0,2:T(8,128)S(1)}) conditional(s32[]{:T(128)} %convert_element_type.66, f32[8,128,128]{1,0,2:T(8,128)S(1)} %get-tuple-element.590, (s32[]{:T(128)}, s32[]{:T(128)}, s32[4,18]{1,0:T(4,128)S(1)}, bf16[4352,128]{1,0:T(8,128)(2,1)S(1)}, bf16[4,18,128,128]{3,2,1,0:T(8,128)(2,1)}, /*index=5*/s32[4,18]{1,0:T(4,128)S(1)}, ...), branch_computations={%region_1.1_spmd, %region_2.2_spmd} | conditional | flops 80347728 | bytes 3474709 | solution.py:96
  41.9 22.6 %while.32 = (s32[]{:T(128)}, bf16[4352,128]{1,0:T(8,128)(2,1)S(1)}, s32[18,2]{0,1:T(2,128)S(1)}, bf16[18,128,128]{2,1,0:T(8,128)(2,1)S(1)}, s32[]{:T(128)}) while((s32[]{:T(128)}, bf16[4352,128]{1,0:T(8,128)(2,1)S(1)}, s32[18,2]{0,1:T(2,128)S(1)}, bf16[18,128,128]{2,1,0:T(8,128)(2,1)S(1)}, s32[]{:T(128)}) %tuple.94), condition=%wide.while_cond, body=%wide.while_body.sunk | while | flops 2 | bytes 65641 | solution.py:16
  64.5 1.6 fusion.10
  66.6 24.9 %conditional.3 = (f32[8,128,128]{1,0,2:T(8,128)S(1)}) conditional(s32[]{:T(128)} %convert_element_type.66, f32[8,128,128]{1,0,2:T(8,128)S(1)} %get-tuple-element.590, (s32[]{:T(128)}, s32[]{:T(128)}, s32[4,18]{1,0:T(4,128)S(1)}, bf16[4352,128]{1,0:T(8,128)(2,1)S(1)}, bf16[4,18,128,128]{3,2,1,0:T(8,128)(2,1)}, /*index=5*/s32[4,18]{1,0:T(4,128)S(1)}, ...), branch_computations={%region_1.1_spmd, %region_2.2_spmd} | conditional | flops 80347728 | bytes 3474709 | solution.py:96
  66.8 22.6 %while.32 = (s32[]{:T(128)}, bf16[4352,128]{1,0:T(8,128)(2,1)S(1)}, s32[18,2]{0,1:T(2,128)S(1)}, bf16[18,128,128]{2,1,0:T(8,128)(2,1)S(1)}, s32[]{:T(128)}) while((s32[]{:T(128)}, bf16[4352,128]{1,0:T(8,128)(2,1)S(1)}, s32[18,2]{0,1:T(2,128)S(1)}, bf16[18,128,128]{2,1,0:T(8,128)(2,1)S(1)}, s32[]{:T(128)}) %tuple.94), condition=%wide.while_cond, body=%wide.while_body.sunk | while | flops 2 | bytes 65641 | solution.py:16
  89.4 1.6 fusion.10
  91.6 24.9 %conditional.3 = (f32[8,128,128]{1,0,2:T(8,128)S(1)}) conditional(s32[]{:T(128)} %convert_element_type.66, f32[8,128,128]{1,0,2:T(8,128)S(1)} %get-tuple-element.590, (s32[]{:T(128)}, s32[]{:T(128)}, s32[4,18]{1,0:T(4,128)S(1)}, bf16[4352,128]{1,0:T(8,128)(2,1)S(1)}, bf16[4,18,128,128]{3,2,1,0:T(8,128)(2,1)}, /*index=5*/s32[4,18]{1,0:T(4,128)S(1)}, ...), branch_computations={%region_1.1_spmd, %region_2.2_spmd} | conditional | flops 80347728 | bytes 3474709 | solution.py:96
  91.7 22.6 %while.32 = (s32[]{:T(128)}, bf16[4352,128]{1,0:T(8,128)(2,1)S(1)}, s32[18,2]{0,1:T(2,128)S(1)}, bf16[18,128,128]{2,1,0:T(8,128)(2,1)S(1)}, s32[]{:T(128)}) while((s32[]{:T(128)}, bf16[4352,128]{1,0:T(8,128)(2,1)S(1)}, s32[18,2]{0,1:T(2,128)S(1)}, bf16[18,128,128]{2,1,0:T(8,128)(2,1)S(1)}, s32[]{:T(128)}) %tuple.94), condition=%wide.while_cond, body=%wide.while_body.sunk | while | flops 2 | bytes 65641 | solution.py:16
  114.4 1.6 fusion.10
  116.5 24.9 %conditional.3 = (f32[8,128,128]{1,0,2:T(8,128)S(1)}) conditional(s32[]{:T(128)} %convert_element_type.66, f32[8,128,128]{1,0,2:T(8,128)S(1)} %get-tuple-element.590, (s32[]{:T(128)}, s32[]{:T(128)}, s32[4,18]{1,0:T(4,128)S(1)}, bf16[4352,128]{1,0:T(8,128)(2,1)S(1)}, bf16[4,18,128,128]{3,2,1,0:T(8,128)(2,1)}, /*index=5*/s32[4,18]{1,0:T(4,128)S(1)}, ...), branch_computations={%region_1.1_spmd, %region_2.2_spmd} | conditional | flops 80347728 | bytes 3474709 | solution.py:96
  116.7 22.6 %while.32 = (s32[]{:T(128)}, bf16[4352,128]{1,0:T(8,128)(2,1)S(1)}, s32[18,2]{0,1:T(2,128)S(1)}, bf16[18,128,128]{2,1,0:T(8,128)(2,1)S(1)}, s32[]{:T(128)}) while((s32[]{:T(128)}, bf16[4352,128]{1,0:T(8,128)(2,1)S(1)}, s32[18,2]{0,1:T(2,128)S(1)}, bf16[18,128,128]{2,1,0:T(8,128)(2,1)S(1)}, s32[]{:T(128)}) %tuple.94), condition=%wide.while_cond, body=%wide.while_body.sunk | while | flops 2 | bytes 65641 | solution.py:16
  139.3 1.6 fusion.10
  141.8 2.5 convert_reduce_fusion
  144.4 0.9 fusion.46
  145.6 20.2 %while.33 = (s32[]{:T(128)}, f32[4,8,128,128]{3,2,1,0:T(8,128)}, s32[4]{0:T(128)S(1)}, s32[]{:T(128)}, s32[4,18]{1,0:T(4,128)S(1)}, /*index=5*/bf16[8,128,128]{2...) while((s32[]{:T(128)}, f32[4,8,128,128]{3,2,1,0:T(8,128)}, ...), condition=%wide.region_5.6_spmd, body=%wide.region_4.5_spmd.sunk | while | flops 80512464 | bytes 6165470 | solution.py:141
  147.0 0.7 gather_fusion
  147.7 1.5 fusion.71
  149.8 0.8 constant_dynamic-update-slice_fusion.2
  152.0 0.7 gather_fusion
  152.7 1.5 fusion.71
  154.9 0.9 constant_dynamic-update-slice_fusion.2
  157.1 0.7 gather_fusion
  157.7 1.5 fusion.71
  159.9 0.9 constant_dynamic-update-slice_fusion.2
  162.1 0.7 gather_fusion
  162.8 1.5 fusion.71
  165.0 0.9 constant_dynamic-update-slice_fusion.2
  166.2 0.8 copy.19
  166.9 3.7 %all-to-all-start.1 = ((bf16[8,48,128]{2,1,0:T(8,128)(2,1)}), bf16[8,48,128]{2,1,0:T(8,128)(2,1)S(1)}, u32[]{:S(2)}, u32[]{:S(2)}) async-start(bf16[8,48,128]{2,1,0:T(8,128)(2,1)} %bitcast.26), calls=%async_computation.2 | async-start | bytes 196608 | tf_op jit(solution)/shard_map/all_to_all | solution.py:116
  170.6 40.6 %psum.15 = f32[256]{0:T(256)S(1)} all-reduce(f32[256]{0:T(256)S(1)} %get-tuple-element.426), channel_id=1, replica_groups=mesh['dom'=8,'blk'=4] {'dom','blk'}, use_global_device_ids=true, to_apply=%region_10.11 | all-reduce | flops 256 | bytes 2048 | tf_op jit(solution)/shard_map/psum | solution.py:146
  211.7 55.9 %all-reduce.3.cloned.1.call-done = f32[128,256]{1,0:T(8,128)} async-done(((f32[128,256]{1,0:T(8,128)}), f32[128,256]{1,0:T(8,128)}) %all-reduce.3.cloned.1.call-update) | async-done | bytes 131088 | tf_op jit(solution)/shard_map/psum | solution.py:146
  267.7 1.6 broadcast_multiply_fusion
  269.4 43.5 %reduce-scatter.2.cloned.1.call-done = f32[1024,128]{1,0:T(8,128)} async-done(((f32[4096,128]{1,0:T(8,128)}), f32[1024,128]{1,0:T(8,128)}) %reduce-scatter.2.cloned.1.call-update) | async-done | bytes 524304 | tf_op jit(solution)/shard_map/reduce_scatter | solution.py:140
  312.9 4.2 %scatter_fusion = f32[1024,128]{1,0:T(8,128)} fusion(f32[1024,128]{1,0:T(8,128)} %reduce-scatter.2.cloned.1.call-done, s32[384]{0:T(512)S(1)} %fusion.45, f32[384,128]{1,0:T(8,128)S(1)} %bitcast.102), kind=kCustom, calls=%fused_computation.2 | custom fusion | flops 49152 | bytes 591360 | tf_op jit(solution)/shard_map/scatter-add | solution.py:127
  317.1 1.8 convert_element_type.50
  (309 shorter events, 99.1 us)
Async XLA Ops:
  7.2 134.2 %copy-start = (bf16[1024,384]{1,0:T(8,128)(2,1)S(1)}, bf16[1024,384]{1,0:T(8,128)(2,1)}, u32[]{:S(2)}) copy-start(bf16[1024,384]{1,0:T(8,128)(2,1)} %param.22) | copy-start | bytes 2359300
  7.2 33.1 %all-gather.2.cloned.1.call-start = ((), (), s32[]{:S(2)}) async-start(), calls=%async_computation.3 | async-start | bytes 1310720 | tf_op jit(solution)/shard_map/all_gather | solution.py:74
  7.9 33.7 %copy-start.2 = (s32[1,4]{1,0:T(1,128)S(1)}, s32[1,4]{1,0:T(1,128)}, u32[]{:S(2)}) copy-start(s32[1,4]{1,0:T(1,128)} %param.21) | copy-start | bytes 52
  13.1 128.3 %all-to-all-start = ((bf16[8,48,128]{2,1,0:T(8,128)(2,1)}), bf16[8,48,128]{2,1,0:T(8,128)(2,1)S(1)}, u32[]{:S(2)}, u32[]{:S(2)}) async-start(bf16[8,48,128]{2,1,0:T(8,128)(2,1)} %select_select_fusion), calls=%async_computation | async-start | bytes 196608 | tf_op jit(solution)/shard_map/all_to_all | solution.py:67
  18.3 249.4 %all-reduce.3.cloned.1.call-start = ((), (), s32[]{:S(2)}) async-start(), calls=%async_computation.5 | async-start | bytes 262144 | tf_op jit(solution)/shard_map/psum | solution.py:146
  41.6 100.2 %copy-start.1 = (bf16[128,256]{1,0:T(8,128)(2,1)S(1)}, bf16[128,256]{1,0:T(8,128)(2,1)}, u32[]{:S(2)}) copy-start(bf16[128,256]{1,0:T(8,128)(2,1)} %param.25) | copy-start | bytes 196612
  41.6 100.2 %copy-start.3 = (f32[256]{0:T(256)S(1)}, f32[256]{0:T(256)}, u32[]{:S(2)}) copy-start(f32[256]{0:T(256)} %param.26) | copy-start | bytes 3076
  145.6 167.3 %reduce-scatter.2.cloned.1.call-start = ((), (), s32[]{:S(2)}) async-start(), calls=%async_computation.4 | async-start | bytes 2621440 | tf_op jit(solution)/shard_map/reduce_scatter | solution.py:140
  166.9 102.3 %all-to-all-start.1 = ((bf16[8,48,128]{2,1,0:T(8,128)(2,1)}), bf16[8,48,128]{2,1,0:T(8,128)(2,1)S(1)}, u32[]{:S(2)}, u32[]{:S(2)}) async-start(bf16[8,48,128]{2,1,0:T(8,128)(2,1)} %bitcast.26), calls=%async_computation.2 | async-start | bytes 196608 | tf_op jit(solution)/shard_map/all_to_all | solution.py:116
Sparse Core Ops, SparseCore 0:
  9.6 30.6 all-gather.1
  145.7 121.9 all-reduce.2
  270.0 42.8 reduce-scatter.1
where the time goes:
time: 327 us; the launch traced here: 325 us
  waiting for transfers between devices  118 us (36%)
  local copies, waits for them, and re-layouts  102 us (31%)
  blocking collectives  40.6 us (12%)
  matrix products  20.5 us (6%)
  other arithmetic  16.4 us (5%)
  between operations  13.9 us (4%)
  starting transfers between devices  8.96 us (3%)
  loops' own time  4.92 us (2%)
    gather x216, local copies, waits for them, and re-layouts  89 us
    psum x1, waiting for transfers between devices, shards(): weight_sum, bias_sum = lax.psum((weight_term, bias_term), ('dom', 'blk'))  55.9 us
    reduce_scatter x1, waiting for transfers between devices, shards(): lax.psum_scatter(lax.map(one_panel, panel_ids).reshape(row_total, feature...  43.5 us
    psum x1, blocking collectives, shards(): weight_sum, bias_sum = lax.psum((weight_term, bias_term), ('dom', 'blk'))  40.6 us
    all_gather x1, waiting for transfers between devices, shards(): piece = lax.all_gather(features, 'blk', axis=0, tiled=True)  17.8 us
    dot_general x16, matrix products, accumulate(): jnp.einsum(pattern, selector, tiles_here, picked, preferred_element_type=...  16 us
  transfers between devices with their start and end apart: 5, of which 3 were waited for; matrix products, arithmetic and copies ran while one was open for 40% of the time, Pallas kernels for 0%

commit v1 on v0

v1 whole, which is shorter than its diff:
```python
import functools
import math

import jax
import jax.numpy as jnp
from jax import lax
from jax.experimental import pallas as pl
from jax.experimental.pallas import tpu as pltpu
from jax.sharding import PartitionSpec as P

MESH = pl.DeviceIdType.MESH
F32 = jnp.float32
BF16 = jnp.bfloat16


def dot(a, b, ca=1, cb=0):
    return lax.dot_general(a, b, (((ca,), (cb,)), ((), ())), preferred_element_type=F32)


def build(counts, rows, cols, send_counts, tiles, send_idx, x, a, picks, outgoing):
    step = pl.program_id(0)
    slots, side, _ = tiles.shape
    dom, most, width = outgoing.shape
    a[...] = jnp.zeros_like(a)

    def add(t, carry):
        r = pl.multiple_of(rows[0, step * slots + t] * side, side)
        c = pl.multiple_of(cols[0, step * slots + t] * side, side)
        a[0, pl.ds(r, side), pl.ds(c, side)] += tiles[t]
        return carry

    lax.fori_loop(0, counts[0, step], add, 0)

    @pl.when(step == 0)
    def _():
        lane = lax.broadcasted_iota(jnp.int32, send_idx.shape, 1)
        index = jnp.full(send_idx.shape, -1, jnp.int32)
        for k in range(dom):
            live = (lane >= k * most) & (lane < k * most + send_counts[0, k])
            index = jnp.where(live, send_idx[...], index)
        row = lax.broadcasted_iota(jnp.int32, picks.shape, 0)
        picks[...] = jnp.where(row == index, 1.0, 0.0).astype(BF16)
        outgoing[...] = dot(picks[...], x[...], 0, 0).astype(BF16).reshape(dom, most, width)


def layer(
    dom, blk, scale,
    a_hbm, x, cut, picks, outgoing, weight, bias, cot,
    y, grad_x, grad_w, grad_b,
    a, panels, received, back, returned, part, part_in, agg, dpre,
    w_out, w_in, w_mid, w_blk, w_all,
    a_sem, xs, xr, cs, cr, bs, br, ps, pr, w1s, w1r, w2s, w2r, w3s, w3r,
):
    g = lax.axis_index("dom")
    b = lax.axis_index("blk")
    rows, width = x.shape
    hidden = weight.shape[1]
    cuts = cut.shape[1]
    share = width // dom

    def load(s):
        return pltpu.make_async_copy(a_hbm.at[s], a.at[s], a_sem.at[s])

    for s in range(blk):
        load(s).start()

    def other(me, n, i):
        return lax.rem(me + i, n)

    barrier = pltpu.get_barrier_semaphore()

    @pl.loop(1, dom)
    def _(i):
        pl.semaphore_signal(barrier, inc=1, device_id=(other(g, dom, i), b), device_id_type=MESH)

    @pl.loop(1, blk)
    def _(i):
        pl.semaphore_signal(barrier, inc=1, device_id=(g, other(b, blk, i)), device_id_type=MESH)

    pl.semaphore_wait(barrier, dom + blk - 2)

    def over_dom(src, dst, ss, rs, peer, slot):
        return pltpu.make_async_remote_copy(
            src, dst, ss.at[peer], rs.at[slot], device_id=(peer, b), device_id_type=MESH
        )

    def over_blk(src, dst, ss, rs, peer, slot):
        return pltpu.make_async_remote_copy(
            src, dst, ss.at[peer], rs.at[slot], device_id=(g, peer), device_id_type=MESH
        )

    def each(n, me, body):
        @pl.loop(1, n)
        def _(i):
            body(other(me, n, i))

    each(blk, b, lambda k: over_blk(x, panels.at[b], xs, xr, k, b).start())
    each(dom, g, lambda k: over_dom(outgoing.at[k], received.at[g], cs, cr, k, g).start())
    received[g] = outgoing[g]

    load(0).wait()
    total = dot(a[0], x[...])
    each(dom, g, lambda k: over_dom(outgoing.at[k], received.at[k], cs, cr, k, k).wait_recv())
    total = total + dot(cut[...], received[...].reshape(cuts, width))

    def gather(s, acc):
        q = lax.rem(b - s + blk, blk)
        over_blk(x, panels.at[q], xs, xr, q, q).wait_recv()
        load(s).wait()
        return acc + dot(a[s], panels[q])

    total = lax.fori_loop(1, blk, gather, total)
    agg[...] = total.astype(BF16)
    bias_sum = jnp.zeros((1, hidden), F32)
    block = 256
    for n in range(rows // block):
        here = pl.ds(n * block, block)
        pre = dot(agg[here, :], weight[...]) + bias[...]
        s = 1.0 / (1.0 + jnp.exp(-pre))
        y[here, :] = (pre * s).astype(BF16)
        d = (cot[here, :].astype(F32) * s * (1.0 + pre * (1.0 - s))).astype(BF16)
        dpre[here, :] = d
        bias_sum = bias_sum + jnp.sum(d.astype(F32), axis=0, keepdims=True)

    dz_t = dot(weight[...], dpre[...], 1, 1).astype(BF16)
    back[...] = dot(dz_t, cut[...]).T.astype(BF16).reshape(back.shape)
    each(dom, g, lambda k: over_dom(back.at[k], returned.at[g], bs, br, k, g).start())
    returned[g] = back[g]

    w_term = dot(agg[...], dpre[...], 0, 0)
    w_out[:, :share, :] = w_term.reshape(dom, share, hidden)
    w_out[:, share:, :] = jnp.broadcast_to(bias_sum[None], (dom, 8, hidden))
    each(dom, g, lambda k: over_dom(w_out.at[k], w_in.at[g], w1s, w1r, k, g).start())
    w_in[g] = w_out[g]

    def spread(i, carry):
        q = lax.rem(b - i + blk, blk)
        part[q] = dot(dz_t, a[i]).astype(BF16)
        over_blk(part.at[q], part_in.at[b], ps, pr, q, b).start()
        return carry

    lax.fori_loop(1, blk, spread, 0)
    mine = dot(dz_t, a[0])

    each(dom, g, lambda k: over_dom(w_out.at[k], w_in.at[k], w1s, w1r, k, k).wait_recv())
    w_mid[...] = jnp.sum(w_in[...], axis=0)
    each(blk, b, lambda k: over_blk(w_mid, w_blk.at[b], w2s, w2r, k, b).start())
    w_blk[b] = w_mid[...]
    each(dom, g, lambda k: over_dom(back.at[k], returned.at[k], bs, br, k, k).wait_recv())
    from_cut = dot(picks[...], returned[...].reshape(cuts, width))
    each(blk, b, lambda k: over_blk(w_mid, w_blk.at[k], w2s, w2r, k, k).wait_recv())
    w_all[g] = jnp.sum(w_blk[...], axis=0) * scale
    each(dom, g, lambda k: over_dom(w_all.at[g], w_all.at[g], w3s, w3r, k, g).start())

    def collect(i, acc):
        q = lax.rem(b + i, blk)
        over_blk(part.at[q], part_in.at[q], ps, pr, q, q).wait_recv()
        return acc + part_in[q].astype(F32)

    mine = lax.fori_loop(1, blk, collect, mine)
    grad_x[...] = (mine.T + from_cut).astype(BF16)

    each(dom, g, lambda k: over_dom(w_all.at[k], w_all.at[k], w3s, w3r, k, k).wait_recv())
    grad_w[...] = w_all[:, :share, :].reshape(width, hidden)
    grad_b[...] = w_all[g, pl.ds(share, 1), :]

    each(blk, b, lambda k: over_blk(x, panels.at[b], xs, xr, k, b).wait_send())
    each(dom, g, lambda k: over_dom(outgoing.at[k], received.at[g], cs, cr, k, g).wait_send())
    each(dom, g, lambda k: over_dom(back.at[k], returned.at[g], bs, br, k, g).wait_send())
    each(dom, g, lambda k: over_dom(w_out.at[k], w_in.at[g], w1s, w1r, k, g).wait_send())
    each(blk, b, lambda k: over_blk(part.at[k], part_in.at[b], ps, pr, k, b).wait_send())
    each(blk, b, lambda k: over_blk(w_mid, w_blk.at[b], w2s, w2r, k, b).wait_send())
    each(dom, g, lambda k: over_dom(w_all.at[g], w_all.at[g], w3s, w3r, k, g).wait_send())


def shards(
    features, tile_vals, tile_rows, tile_cols, tile_count, cut_weights,
    send_idx, send_count, weight, bias, cotangent,
):
    rows, width = features.shape
    side = tile_vals.shape[1]
    blk = lax.axis_size("blk")
    dom = lax.axis_size("dom")
    slots = tile_vals.shape[0] // blk
    cuts = send_idx.shape[1]
    most = cuts // dom
    hidden = weight.shape[1]
    smem = pl.BlockSpec(memory_space=pltpu.SMEM)
    vmem = pl.BlockSpec(memory_space=pltpu.VMEM)
    whole = lambda *shape: pl.BlockSpec(shape, lambda s: (0,) * len(shape))
    a, picks, outgoing = pl.pallas_call(
        build,
        grid=(blk,),
        out_shape=(
            jax.ShapeDtypeStruct((blk, rows, rows), BF16),
            jax.ShapeDtypeStruct((rows, cuts), BF16),
            jax.ShapeDtypeStruct((dom, most, width), BF16),
        ),
        in_specs=[smem, smem, smem, smem,
                  pl.BlockSpec((slots, side, side), lambda s: (s, 0, 0)),
                  whole(1, cuts), whole(rows, width)],
        out_specs=(pl.BlockSpec((1, rows, rows), lambda s: (s, 0, 0)),
                   whole(rows, cuts), whole(dom, most, width)),
        compiler_params=pltpu.CompilerParams(vmem_limit_bytes=40 << 20),
    )(tile_count, tile_rows, tile_cols, send_count, tile_vals, send_idx, features)

    share = width // dom
    piece = share + 8
    dma = pltpu.SemaphoreType.DMA
    over_d, over_b = dma((dom,)), dma((blk,))
    y, grad_x, grad_w, grad_b = pl.pallas_call(
        functools.partial(layer, dom, blk, 1.0 / math.sqrt(dom * blk * rows)),
        out_shape=(
            jax.ShapeDtypeStruct((rows, hidden), BF16),
            jax.ShapeDtypeStruct((rows, width), BF16),
            jax.ShapeDtypeStruct((width, hidden), F32),
            jax.ShapeDtypeStruct((1, hidden), F32),
        ),
        in_specs=[pl.BlockSpec(memory_space=pl.ANY)] + [vmem] * 7,
        out_specs=(vmem,) * 4,
        scratch_shapes=[
            pltpu.VMEM((blk, rows, rows), BF16),
            pltpu.VMEM((blk, rows, width), BF16),
            pltpu.VMEM((dom, most, width), BF16),
            pltpu.VMEM((dom, most, width), BF16),
            pltpu.VMEM((dom, most, width), BF16),
            pltpu.VMEM((blk, width, rows), BF16),
            pltpu.VMEM((blk, width, rows), BF16),
            pltpu.VMEM((rows, width), BF16),
            pltpu.VMEM((rows, hidden), BF16),
            pltpu.VMEM((dom, piece, hidden), F32),
            pltpu.VMEM((dom, piece, hidden), F32),
            pltpu.VMEM((piece, hidden), F32),
            pltpu.VMEM((blk, piece, hidden), F32),
            pltpu.VMEM((dom, piece, hidden), F32),
            over_b, over_b, over_b, over_d, over_d, over_d, over_d,
            over_b, over_b, over_d, over_d, over_b, over_b, over_d, over_d,
        ],
        compiler_params=pltpu.CompilerParams(
            collective_id=0, has_side_effects=True, vmem_limit_bytes=60 << 20
        ),
    )(a, features, cut_weights, picks, outgoing, weight, bias.reshape(1, hidden), cotangent)
    return y, grad_x, grad_w, grad_b.reshape(hidden)


def solution(mesh):
    split = P(("dom", "blk"), None)
    in_specs = (
        split, P(("dom", "blk"), None, None), split, split, split, split, split, split,
        P(), P(), split,
    )
    out_specs = (split, split, P(), P())
    return jax.shard_map(shards, mesh=mesh, in_specs=in_specs, out_specs=out_specs, check_vma=False)
```

time: 327 us -> 82.9 us (0.25)
  waiting for transfers between devices: 118 us -> 0 us
  local copies, waits for them, and re-layouts: 102 us -> 17 us
  Pallas kernels: 0 us -> 63.8 us
  blocking collectives: 40.6 us -> 0 us
  matrix products: 20.5 us -> 0 us
  other arithmetic: 16.4 us -> 0 us
  between operations: 13.9 us -> 0.68 us
  starting transfers between devices: 8.96 us -> 0 us
  loops' own time: 4.92 us -> 0 us
    gather x221 -> x0, local copies, waits for them, and re-layouts: 93.8 us -> none
    pallas_call x0 -> x2, Pallas kernels: none -> 63.8 us  [the longest x1 61.6 us: shards(): pl.pallas_call(functools.partial(layer, dom, blk, 1.0 / math.sqrt(dom * b...]
    psum x1 -> x0, waiting for transfers between devices: 55.9 us -> none  [shards(): weight_sum, bias_sum = lax.psum((weight_term, bias_term), ('dom', 'blk'))]
    reduce_scatter x1 -> x0, waiting for transfers between devices: 43.5 us -> none  [shards(): lax.psum_scatter(lax.map(one_panel, panel_ids).reshape(row_total, feature...]
    psum x1 -> x0, blocking collectives: 40.6 us -> none  [shards(): weight_sum, bias_sum = lax.psum((weight_term, bias_term), ('dom', 'blk'))]
    dot_general x21 -> x0, matrix products: 20.5 us -> none  [the longest x16 16 us: accumulate(): jnp.einsum(pattern, selector, tiles_here, picked, preferred_element_type=...]
    all_gather x1 -> x0, waiting for transfers between devices: 17.8 us -> none  [shards(): piece = lax.all_gather(features, 'blk', axis=0, tiled=True)]
    unnamed x9 -> x24, local copies, waits for them, and re-layouts: 0.54 us -> 17 us
  transfers between devices with their start and end apart: 5 -> 0, of which waited for: 3 -> 0; matrix products, arithmetic and copies ran while one was open for 40% -> 0% of each run, Pallas kernels for 0% -> 0%
where the time goes in v1:
time: 82.9 us; the launch traced here: 81.5 us
  Pallas kernels  63.8 us (77%)
  local copies, waits for them, and re-layouts  17 us (21%)
    pallas_call x1, Pallas kernels, shards(): pl.pallas_call(functools.partial(layer, dom, blk, 1.0 / math.sqrt(dom * b...  61.6 us
    unnamed x24, local copies, waits for them, and re-layouts  17 us
    pallas_call x1, Pallas kernels, shards(): pl.pallas_call(build, grid=(blk,), out_shape=(jax.ShapeDtypeStruct((blk,...  2.25 us

profile of v1, /device:TPU:0, one launch (start us, length us, event | category | flops | bytes accessed | tf_op | source)
XLA Modules:
  0.0 81.5 jit_solution(16881377024584175693)
XLA Ops:
  0.6 0.0 copy-start.1
  0.6 1.7 %copy-done.1 = bf16[72,128,128]{2,1,0:T(8,128)(2,1)S(1)} copy-done((bf16[72,128,128]{2,1,0:T(8,128)(2,1)S(1)}, bf16[72,128,128]{2,1,0:T(8,128)(2,1)}, u32[]{:S(2)}) %copy-start.1) | copy-done | bytes 2359320
  2.3 0.0 copy-start.2
  2.3 0.9 %copy-done.2 = bf16[1024,128]{1,0:T(8,128)(2,1)S(1)} copy-done((bf16[1024,128]{1,0:T(8,128)(2,1)S(1)}, bf16[1024,128]{1,0:T(8,128)(2,1)}, u32[]{:S(2)}) %copy-start.2) | copy-done | bytes 262168
  3.2 0.0 copy-start.5
  3.3 0.7 copy-done.5
  3.9 0.0 copy-start.6
  3.9 0.7 copy-done.6
  4.6 0.0 copy-start.7
  4.6 0.7 copy-done.7
  5.2 0.0 copy-start.8
  5.2 0.7 copy-done.8
  5.9 0.0 copy-start.9
  5.9 0.7 copy-done.9
  6.6 2.2 %shard_map.138 = (bf16[4,1024,1024]{2,1,0:T(8,128)(2,1)S(1)}, bf16[1024,384]{1,0:T(8,128)(2,1)S(1)}, bf16[8,48,128]{2,1,0:T(8,128)(2,1)S(1)}) custom-call(s32[1,4]{1,0:T(1,128)S(1)} %copy-done.6, s32[1,72]{1,0:T(1,128)S(1)} %copy-done.7, s32[1,72]{1,0:T(1,128)S(1)} %copy-done.8, s32[1,8]{1,0:T(1,128)S(1)} %copy-done.9, bf16[72,128,128]{2,1,0:T(8,128)(2,1)S(1)} %copy-done.1, ...), custom_call_target="tpu_custom_call" | custom-call | tf_op jit(solution)/shard_map/pallas_call | solution.py:191
  8.8 0.0 copy-start
  8.8 3.2 %copy-done = bf16[4,1024,1024]{2,1,0:T(8,128)(2,1)} copy-done((bf16[4,1024,1024]{2,1,0:T(8,128)(2,1)}, bf16[4,1024,1024]{2,1,0:T(8,128)(2,1)S(1)}, u32[]{:S(2)}) %copy-start) | copy-done | bytes 8388632
  12.0 0.0 copy-start.3
  12.0 1.0 %copy-done.3 = bf16[1024,384]{1,0:T(8,128)(2,1)} copy-done((bf16[1024,384]{1,0:T(8,128)(2,1)}, bf16[1024,384]{1,0:T(8,128)(2,1)S(1)}, u32[]{:S(2)}) %copy-start.3) | copy-done | bytes 786456
  13.0 0.0 copy-start.4
  13.0 0.6 copy-done.4
  13.6 61.6 %shard_map.139 = (bf16[1024,256]{1,0:T(8,128)(2,1)}, bf16[1024,128]{1,0:T(8,128)(2,1)}, f32[128,256]{1,0:T(8,128)}, f32[1,256]{1,0:T(1,128)}) custom-call(bf16[4,1024,1024]{2,1,0:T(8,128)(2,1)} %copy-done, bf16[1024,128]{1,0:T(8,128)(2,1)} %x.3, bf16[1024,384]{1,0:T(8,128)(2,1)} %cut.1, bf16[1024,384]{1,0:T(8,128)(2,1)} %copy-done.3, ...), custom_call_target="tpu_custom_call" | custom-call | tf_op jit(solution)/shard_map/pallas_call | solution.py:211
  75.2 1.9 %copy.19 = bf16[1024,256]{1,0:T(8,128)(2,1)} copy(bf16[1024,256]{1,0:T(8,128)(2,1)} %get-tuple-element.22) | data formatting | bytes 1048576
  77.1 1.7 %copy.20 = bf16[1024,128]{1,0:T(8,128)(2,1)} copy(bf16[1024,128]{1,0:T(8,128)(2,1)} %get-tuple-element.23) | data formatting | bytes 524288
  78.7 1.6 %copy.21 = f32[128,256]{1,0:T(8,128)} copy(f32[128,256]{1,0:T(8,128)} %get-tuple-element.24) | data formatting | bytes 262144
  80.3 1.2 %copy.22 = f32[256]{0:T(256)} copy(f32[256]{0:T(256)} %bitcast.3) | data formatting | bytes 2048
Async XLA Ops:
  0.6 1.7 %copy-start.1 = (bf16[72,128,128]{2,1,0:T(8,128)(2,1)S(1)}, bf16[72,128,128]{2,1,0:T(8,128)(2,1)}, u32[]{:S(2)}) copy-start(bf16[72,128,128]{2,1,0:T(8,128)(2,1)} %tiles.1) | copy-start | bytes 7077892
  2.3 0.9 %copy-start.2 = (bf16[1024,128]{1,0:T(8,128)(2,1)S(1)}, bf16[1024,128]{1,0:T(8,128)(2,1)}, u32[]{:S(2)}) copy-start(bf16[1024,128]{1,0:T(8,128)(2,1)} %x.3) | copy-start | bytes 786436
  3.2 0.7 copy-start.5
  3.9 0.7 copy-start.6
  4.6 0.7 copy-start.7
  5.2 0.7 copy-start.8
  5.9 0.7 copy-start.9
  8.8 3.2 %copy-start = (bf16[4,1024,1024]{2,1,0:T(8,128)(2,1)}, bf16[4,1024,1024]{2,1,0:T(8,128)(2,1)S(1)}, u32[]{:S(2)}) copy-start(bf16[4,1024,1024]{2,1,0:T(8,128)(2,1)S(1)} %get-tuple-element.11.a_hbm) | copy-start | bytes 25165828
  12.0 1.0 %copy-start.3 = (bf16[1024,384]{1,0:T(8,128)(2,1)}, bf16[1024,384]{1,0:T(8,128)(2,1)S(1)}, u32[]{:S(2)}) copy-start(bf16[1024,384]{1,0:T(8,128)(2,1)S(1)} %get-tuple-element.12.picks) | copy-start | bytes 2359300
  13.0 0.6 copy-start.4

commit v2 on v1

--- a/solution.py
+++ b/solution.py
@@ -45,11 +45,13 @@
 
 def layer(
     dom, blk, scale,
-    a_hbm, x, cut, picks, outgoing, weight, bias, cot,
+    a_hbm, x, cut_hbm, picks_hbm, outgoing, weight_hbm, bias, cot_hbm,
     y, grad_x, grad_w, grad_b,
-    a, panels, received, back, returned, part, part_in, agg, dpre,
+    a, cut, picks, weight, cot,
+    panels, received, back, returned, part, from_low, from_high, total, agg, dpre,
     w_out, w_in, w_mid, w_blk, w_all,
-    a_sem, xs, xr, cs, cr, bs, br, ps, pr, w1s, w1r, w2s, w2r, w3s, w3r,
+    a_sem, o_sem, up_s, up_r, dn_s, dn_r, cs, cr, bs, br,
+    pu_s, pu_r, pd_s, pd_r, w1s, w1r, w2s, w2r, w3s, w3r,
 ):
     g = lax.axis_index("dom")
     b = lax.axis_index("blk")
@@ -57,12 +59,23 @@
     hidden = weight.shape[1]
     cuts = cut.shape[1]
     share = width // dom
+    last = blk - 1
 
     def load(s):
         return pltpu.make_async_copy(a_hbm.at[s], a.at[s], a_sem.at[s])
 
-    for s in range(blk):
+    operands = [
+        pltpu.make_async_copy(src, dst, o_sem.at[n])
+        for n, (src, dst) in enumerate(
+            ((cut_hbm, cut), (weight_hbm, weight), (cot_hbm, cot), (picks_hbm, picks))
+        )
+    ]
+    load(0).start()
+    operands[0].start()
+    for s in range(1, blk):
         load(s).start()
+    for copy in operands[1:]:
+        copy.start()
 
     def other(me, n, i):
         return lax.rem(me + i, n)
@@ -84,9 +97,9 @@
             src, dst, ss.at[peer], rs.at[slot], device_id=(peer, b), device_id_type=MESH
         )
 
-    def over_blk(src, dst, ss, rs, peer, slot):
+    def over_blk(src, dst, ss, rs, peer, send, slot):
         return pltpu.make_async_remote_copy(
-            src, dst, ss.at[peer], rs.at[slot], device_id=(g, peer), device_id_type=MESH
+            src, dst, ss.at[send], rs.at[slot], device_id=(g, peer), device_id_type=MESH
         )
 
     def each(n, me, body):
@@ -94,23 +107,52 @@
         def _(i):
             body(other(me, n, i))
 
-    each(blk, b, lambda k: over_blk(x, panels.at[b], xs, xr, k, b).start())
+    def up(q):
+        return over_blk(panels.at[q], panels.at[q], up_s, up_r, jnp.minimum(b + 1, last), q, q)
+
+    def down(q):
+        return over_blk(panels.at[q], panels.at[q], dn_s, dn_r, jnp.maximum(b - 1, 0), q, q)
+
+    panels[b] = x[...]
+    pl.when(b < last)(lambda: up(b).start())
+    pl.when(b > 0)(lambda: down(b).start())
     each(dom, g, lambda k: over_dom(outgoing.at[k], received.at[g], cs, cr, k, g).start())
     received[g] = outgoing[g]
 
     load(0).wait()
-    total = dot(a[0], x[...])
+    total[...] = dot(a[0], x[...])
+    operands[0].wait()
     each(dom, g, lambda k: over_dom(outgoing.at[k], received.at[k], cs, cr, k, k).wait_recv())
-    total = total + dot(cut[...], received[...].reshape(cuts, width))
-
-    def gather(s, acc):
-        q = lax.rem(b - s + blk, blk)
-        over_blk(x, panels.at[q], xs, xr, q, q).wait_recv()
+    total[...] += dot(cut[...], received[...].reshape(cuts, width))
+
+    for s in range(1, blk):
         load(s).wait()
-        return acc + dot(a[s], panels[q])
-
-    total = lax.fori_loop(1, blk, gather, total)
-    agg[...] = total.astype(BF16)
+
+    @pl.loop(1, blk)
+    def _(r):
+        low, high = b - r, b + r
+
+        @pl.when(low >= 0)
+        def _():
+            up(low).wait_recv()
+            pl.when(b < last)(lambda: up(low).start())
+
+        @pl.when(high <= last)
+        def _():
+            down(high).wait_recv()
+            pl.when(b > 0)(lambda: down(high).start())
+
+        @pl.when(low >= 0)
+        def _():
+            total[...] += dot(a[r], panels[low])
+
+        @pl.when(high <= last)
+        def _():
+            total[...] += dot(a[blk - r], panels[high])
+
+    agg[...] = total[...].astype(BF16)
+    for copy in operands[1:]:
+        copy.wait()
     bias_sum = jnp.zeros((1, hidden), F32)
     block = 256
     for n in range(rows // block):
@@ -123,6 +165,49 @@
         bias_sum = bias_sum + jnp.sum(d.astype(F32), axis=0, keepdims=True)
 
     dz_t = dot(weight[...], dpre[...], 1, 1).astype(BF16)
+
+    def to_high(q):
+        return over_blk(part.at[q], from_low.at[q], pu_s, pu_r, jnp.minimum(b + 1, last), q, q)
+
+    def to_low(q):
+        return over_blk(part.at[q], from_high.at[q], pd_s, pd_r, jnp.maximum(b - 1, 0), q, q)
+
+    def relay(t):
+        high = last - t + b
+        low = t - last + b
+
+        @pl.when((t >= b) & (high > b))
+        def _():
+            term = dot(dz_t, a[b - high + blk])
+
+            @pl.when(b > 0)
+            def _():
+                to_high(high).wait_recv()
+                part[high] = (term + from_low[high].astype(F32)).astype(BF16)
+
+            @pl.when(b == 0)
+            def _():
+                part[high] = term.astype(BF16)
+
+            to_high(high).start()
+
+        @pl.when((low >= 0) & (low < b))
+        def _():
+            term = dot(dz_t, a[b - low])
+
+            @pl.when(b < last)
+            def _():
+                to_low(low).wait_recv()
+                part[low] = (term + from_high[low].astype(F32)).astype(BF16)
+
+            @pl.when(b == last)
+            def _():
+                part[low] = term.astype(BF16)
+
+            to_low(low).start()
+
+    relay(0)
+
     back[...] = dot(dz_t, cut[...]).T.astype(BF16).reshape(back.shape)
     each(dom, g, lambda k: over_dom(back.at[k], returned.at[g], bs, br, k, g).start())
     returned[g] = back[g]
@@ -133,44 +218,67 @@
     each(dom, g, lambda k: over_dom(w_out.at[k], w_in.at[g], w1s, w1r, k, g).start())
     w_in[g] = w_out[g]
 
-    def spread(i, carry):
-        q = lax.rem(b - i + blk, blk)
-        part[q] = dot(dz_t, a[i]).astype(BF16)
-        over_blk(part.at[q], part_in.at[b], ps, pr, q, b).start()
-        return carry
-
-    lax.fori_loop(1, blk, spread, 0)
     mine = dot(dz_t, a[0])
 
+    def share_w(peer, slot):
+        return over_blk(w_mid, w_blk.at[slot], w2s, w2r, peer, peer, slot)
+
+    pl.loop(1, max(last - 1, 1))(relay)
     each(dom, g, lambda k: over_dom(w_out.at[k], w_in.at[k], w1s, w1r, k, k).wait_recv())
     w_mid[...] = jnp.sum(w_in[...], axis=0)
-    each(blk, b, lambda k: over_blk(w_mid, w_blk.at[b], w2s, w2r, k, b).start())
+    each(blk, b, lambda k: share_w(k, b).start())
     w_blk[b] = w_mid[...]
+    pl.loop(max(last - 1, 1), last)(relay)
+
     each(dom, g, lambda k: over_dom(back.at[k], returned.at[k], bs, br, k, k).wait_recv())
     from_cut = dot(picks[...], returned[...].reshape(cuts, width))
-    each(blk, b, lambda k: over_blk(w_mid, w_blk.at[k], w2s, w2r, k, k).wait_recv())
+    each(blk, b, lambda k: share_w(k, k).wait_recv())
     w_all[g] = jnp.sum(w_blk[...], axis=0) * scale
     each(dom, g, lambda k: over_dom(w_all.at[g], w_all.at[g], w3s, w3r, k, g).start())
 
-    def collect(i, acc):
-        q = lax.rem(b + i, blk)
-        over_blk(part.at[q], part_in.at[q], ps, pr, q, q).wait_recv()
-        return acc + part_in[q].astype(F32)
-
-    mine = lax.fori_loop(1, blk, collect, mine)
-    grad_x[...] = (mine.T + from_cut).astype(BF16)
+    grad = mine.T + from_cut
+    total[...] = grad
+
+    @pl.when(b > 0)
+    def _():
+        to_high(b).wait_recv()
+        total[...] += from_low[b].astype(F32).T
+
+    @pl.when(b < last)
+    def _():
+        to_low(b).wait_recv()
+        total[...] += from_high[b].astype(F32).T
+
+    grad_x[...] = total[...].astype(BF16)
 
     each(dom, g, lambda k: over_dom(w_all.at[k], w_all.at[k], w3s, w3r, k, k).wait_recv())
     grad_w[...] = w_all[:, :share, :].reshape(width, hidden)
     grad_b[...] = w_all[g, pl.ds(share, 1), :]
 
-    each(blk, b, lambda k: over_blk(x, panels.at[b], xs, xr, k, b).wait_send())
+    @pl.loop(0, blk)
+    def _(q):
+        pl.when((b < last) & (q <= b))(lambda: up(q).wait_send())
+        pl.when((b > 0) & (q >= b))(lambda: down(q).wait_send())
+        pl.when(q > b)(lambda: to_high(q).wait_send())
+        pl.when(q < b)(lambda: to_low(q).wait_send())
+
     each(dom, g, lambda k: over_dom(outgoing.at[k], received.at[g], cs, cr, k, g).wait_send())
     each(dom, g, lambda k: over_dom(back.at[k], returned.at[g], bs, br, k, g).wait_send())
     each(dom, g, lambda k: over_dom(w_out.at[k], w_in.at[g], w1s, w1r, k, g).wait_send())
-    each(blk, b, lambda k: over_blk(part.at[k], part_in.at[b], ps, pr, k, b).wait_send())
-    each(blk, b, lambda k: over_blk(w_mid, w_blk.at[b], w2s, w2r, k, b).wait_send())
+    each(blk, b, lambda k: share_w(k, b).wait_send())
     each(dom, g, lambda k: over_dom(w_all.at[g], w_all.at[g], w3s, w3r, k, g).wait_send())
+
+
+def deliver(*refs):
+    count = len(refs) // 2
+    sems = refs[-1]
+    copies = [
+        pltpu.make_async_copy(refs[n], refs[count + n], sems.at[n]) for n in range(count)
+    ]
+    for copy in copies:
+        copy.start()
+    for copy in copies:
+        copy.wait()
 
 
 def shards(
@@ -201,31 +309,39 @@
                   whole(1, cuts), whole(rows, width)],
         out_specs=(pl.BlockSpec((1, rows, rows), lambda s: (s, 0, 0)),
                    whole(rows, cuts), whole(dom, most, width)),
-        compiler_params=pltpu.CompilerParams(vmem_limit_bytes=40 << 20),
+        compiler_params=pltpu.CompilerParams(vmem_limit_bytes=60 << 20),
     )(tile_count, tile_rows, tile_cols, send_count, tile_vals, send_idx, features)
 
     share = width // dom
     piece = share + 8
     dma = pltpu.SemaphoreType.DMA
     over_d, over_b = dma((dom,)), dma((blk,))
-    y, grad_x, grad_w, grad_b = pl.pallas_call(
+    hbm = pl.BlockSpec(memory_space=pl.ANY)
+    shapes = (
+        jax.ShapeDtypeStruct((rows, hidden), BF16),
+        jax.ShapeDtypeStruct((rows, width), BF16),
+        jax.ShapeDtypeStruct((width, hidden), F32),
+        jax.ShapeDtypeStruct((1, hidden), F32),
+    )
+    results = pl.pallas_call(
         functools.partial(layer, dom, blk, 1.0 / math.sqrt(dom * blk * rows)),
-        out_shape=(
-            jax.ShapeDtypeStruct((rows, hidden), BF16),
-            jax.ShapeDtypeStruct((rows, width), BF16),
-            jax.ShapeDtypeStruct((width, hidden), F32),
-            jax.ShapeDtypeStruct((1, hidden), F32),
-        ),
-        in_specs=[pl.BlockSpec(memory_space=pl.ANY)] + [vmem] * 7,
+        out_shape=shapes,
+        in_specs=[hbm, vmem, hbm, hbm, vmem, hbm, vmem, hbm],
         out_specs=(vmem,) * 4,
         scratch_shapes=[
             pltpu.VMEM((blk, rows, rows), BF16),
+            pltpu.VMEM((rows, cuts), BF16),
+            pltpu.VMEM((rows, cuts), BF16),
+            pltpu.VMEM((width, hidden), BF16),
+            pltpu.VMEM((rows, hidden), BF16),
             pltpu.VMEM((blk, rows, width), BF16),
             pltpu.VMEM((dom, most, width), BF16),
             pltpu.VMEM((dom, most, width), BF16),
             pltpu.VMEM((dom, most, width), BF16),
             pltpu.VMEM((blk, width, rows), BF16),
             pltpu.VMEM((blk, width, rows), BF16),
+            pltpu.VMEM((blk, width, rows), BF16),
+            pltpu.VMEM((rows, width), F32),
             pltpu.VMEM((rows, width), BF16),
             pltpu.VMEM((rows, hidden), BF16),
             pltpu.VMEM((dom, piece, hidden), F32),
@@ -233,13 +349,20 @@
             pltpu.VMEM((piece, hidden), F32),
             pltpu.VMEM((blk, piece, hidden), F32),
             pltpu.VMEM((dom, piece, hidden), F32),
-            over_b, over_b, over_b, over_d, over_d, over_d, over_d,
-            over_b, over_b, over_d, over_d, over_b, over_b, over_d, over_d,
+            over_b, dma((4,)), over_b, over_b, over_b, over_b, over_d, over_d, over_d, over_d,
+            over_b, over_b, over_b, over_b, over_d, over_d, over_b, over_b, over_d, over_d,
         ],
         compiler_params=pltpu.CompilerParams(
             collective_id=0, has_side_effects=True, vmem_limit_bytes=60 << 20
         ),
     )(a, features, cut_weights, picks, outgoing, weight, bias.reshape(1, hidden), cotangent)
+    y, grad_x, grad_w, grad_b = pl.pallas_call(
+        deliver,
+        out_shape=shapes,
+        in_specs=[hbm] * 4,
+        out_specs=(hbm,) * 4,
+        scratch_shapes=[dma((4,))],
+    )(*results)
     return y, grad_x, grad_w, grad_b.reshape(hidden)
 
 

time: 82.9 us -> 90.1 us (1.087)
  Pallas kernels: 63.8 us -> 88.1 us
  local copies, waits for them, and re-layouts: 17 us -> 0 us
    pallas_call x0 -> x1, Pallas kernels: none -> 29 us  [shards(): pl.pallas_call(deliver, out_shape=shapes, in_specs=[hbm] * 4, out_specs=(...]
    unnamed x24 -> x0, local copies, waits for them, and re-layouts: 17 us -> none
    pallas_call x1, Pallas kernels: 61.6 us -> 52.5 us  [shards(): pl.pallas_call(functools.partial(layer, dom, blk, 1.0 / math.sqrt(dom * b...]
    pallas_call x1, Pallas kernels: 2.25 us -> 6.7 us  [shards(): pl.pallas_call(build, grid=(blk,), out_shape=(jax.ShapeDtypeStruct((blk,...]
where the time goes in v2:
time: 90.1 us; the launch traced here: 88.8 us
  Pallas kernels  88.1 us (98%)
    pallas_call x1, Pallas kernels, shards(): pl.pallas_call(functools.partial(layer, dom, blk, 1.0 / math.sqrt(dom * b...  52.5 us
    pallas_call x1, Pallas kernels, shards(): pl.pallas_call(deliver, out_shape=shapes, in_specs=[hbm] * 4, out_specs=(...  29 us
    pallas_call x1, Pallas kernels, shards(): pl.pallas_call(build, grid=(blk,), out_shape=(jax.ShapeDtypeStruct((blk,...  6.7 us

profile of v2, /device:TPU:0, one launch (start us, length us, event | category | flops | bytes accessed | tf_op | source)
XLA Modules:
  0.0 88.8 jit_solution(10013482177955248350)
XLA Ops:
  0.6 6.7 %shard_map.138 = (bf16[4,1024,1024]{2,1,0:T(8,128)(2,1)}, bf16[1024,384]{1,0:T(8,128)(2,1)}, bf16[8,48,128]{2,1,0:T(8,128)(2,1)}) custom-call(s32[1,4]{1,0:T(1,128)} %counts.1, s32[1,72]{1,0:T(1,128)} %rows.1, s32[1,72]{1,0:T(1,128)} %cols.1, s32[1,8]{1,0:T(1,128)} %send_counts.1, bf16[72,128,128]{2,1,0:T(8,128)(2,1)} %tiles.1, s32[1,384]{1,0:T(1,128)} %send_idx.1, ...), custom_call_target="tpu_custom_call" | custom-call | tf_op jit(solution)/shard_map/pallas_call | solution.py:299
  7.3 52.5 %shard_map.139 = (bf16[1024,256]{1,0:T(8,128)(2,1)}, bf16[1024,128]{1,0:T(8,128)(2,1)}, f32[128,256]{1,0:T(8,128)}, f32[1,256]{1,0:T(1,128)}) custom-call(bf16[4,1024,1024]{2,1,0:T(8,128)(2,1)} %get-tuple-element.15.a_hbm, bf16[1024,128]{1,0:T(8,128)(2,1)} %x.3, bf16[1024,384]{1,0:T(8,128)(2,1)} %cut_hbm.1, bf16[1024,384]{1,0:T(8,128)(2,1)} %get-tuple-element.16.picks_hbm, ...), custom_call_target="tpu_custom_call" | custom-call | tf_op jit(solution)/shard_map/pallas_call | solution.py:326
  59.8 29.0 %shard_map.140 = (bf16[1024,256]{1,0:T(8,128)(2,1)}, bf16[1024,128]{1,0:T(8,128)(2,1)}, f32[128,256]{1,0:T(8,128)}, f32[1,256]{1,0:T(1,128)}) custom-call(bf16[1024,256]{1,0:T(8,128)(2,1)} %get-tuple-element.18.refs_0_, bf16[1024,128]{1,0:T(8,128)(2,1)} %get-tuple-element.19.refs_1_, f32[128,256]{1,0:T(8,128)} %get-tuple-element.20.refs_2_, ...), custom_call_target="tpu_custom_call" | custom-call | tf_op jit(solution)/shard_map/pallas_call | solution.py:359

commit v3 on v2

--- a/solution.py
+++ b/solution.py
@@ -223,21 +223,23 @@
     def share_w(peer, slot):
         return over_blk(w_mid, w_blk.at[slot], w2s, w2r, peer, peer, slot)
 
-    pl.loop(1, max(last - 1, 1))(relay)
     each(dom, g, lambda k: over_dom(w_out.at[k], w_in.at[k], w1s, w1r, k, k).wait_recv())
     w_mid[...] = jnp.sum(w_in[...], axis=0)
     each(blk, b, lambda k: share_w(k, b).start())
     w_blk[b] = w_mid[...]
-    pl.loop(max(last - 1, 1), last)(relay)
-
-    each(dom, g, lambda k: over_dom(back.at[k], returned.at[k], bs, br, k, k).wait_recv())
-    from_cut = dot(picks[...], returned[...].reshape(cuts, width))
+    pl.loop(1, min(2, last))(relay)
+
     each(blk, b, lambda k: share_w(k, k).wait_recv())
     w_all[g] = jnp.sum(w_blk[...], axis=0) * scale
     each(dom, g, lambda k: over_dom(w_all.at[g], w_all.at[g], w3s, w3r, k, g).start())
-
-    grad = mine.T + from_cut
-    total[...] = grad
+    pl.loop(2, last)(relay)
+
+    each(dom, g, lambda k: over_dom(back.at[k], returned.at[k], bs, br, k, k).wait_recv())
+    from_cut = dot(picks[...], returned[...].reshape(cuts, width))
+    total[...] = mine.T + from_cut
+    each(dom, g, lambda k: over_dom(w_all.at[k], w_all.at[k], w3s, w3r, k, k).wait_recv())
+    grad_w[...] = w_all[:, :share, :].reshape(width, hidden)
+    grad_b[...] = w_all[g, pl.ds(share, 1), :]
 
     @pl.when(b > 0)
     def _():
@@ -250,10 +252,6 @@
         total[...] += from_high[b].astype(F32).T
 
     grad_x[...] = total[...].astype(BF16)
-
-    each(dom, g, lambda k: over_dom(w_all.at[k], w_all.at[k], w3s, w3r, k, k).wait_recv())
-    grad_w[...] = w_all[:, :share, :].reshape(width, hidden)
-    grad_b[...] = w_all[g, pl.ds(share, 1), :]
 
     @pl.loop(0, blk)
     def _(q):
@@ -271,14 +269,8 @@
 
 def deliver(*refs):
     count = len(refs) // 2
-    sems = refs[-1]
-    copies = [
-        pltpu.make_async_copy(refs[n], refs[count + n], sems.at[n]) for n in range(count)
-    ]
-    for copy in copies:
-        copy.start()
-    for copy in copies:
-        copy.wait()
+    for n in range(count):
+        refs[count + n][...] = refs[n][...]
 
 
 def shards(
@@ -359,9 +351,9 @@
     y, grad_x, grad_w, grad_b = pl.pallas_call(
         deliver,
         out_shape=shapes,
-        in_specs=[hbm] * 4,
-        out_specs=(hbm,) * 4,
-        scratch_shapes=[dma((4,))],
+        in_specs=[vmem] * 4,
+        out_specs=(vmem,) * 4,
+        compiler_params=pltpu.CompilerParams(vmem_limit_bytes=60 << 20),
     )(*results)
     return y, grad_x, grad_w, grad_b.reshape(hidden)
 

time: 90.1 us -> 62.9 us (0.70); the launches traced: 88.8 us -> 62.7 us
  Pallas kernels: 88.1 us -> 62 us
    pallas_call x1, Pallas kernels: 29 us -> 2.08 us  [shards(): pl.pallas_call(deliver, out_shape=shapes, in_specs=[vmem] * 4, out_specs=...]
    pallas_call x1, Pallas kernels: 52.5 us -> 53.4 us  [shards(): pl.pallas_call(functools.partial(layer, dom, blk, 1.0 / math.sqrt(dom * b...]
where the time goes in v3:
time: 62.9 us; the launch traced here: 62.7 us
  Pallas kernels  62 us (99%)
  between operations  0.64 us (1%)
    pallas_call x1, Pallas kernels, shards(): pl.pallas_call(functools.partial(layer, dom, blk, 1.0 / math.sqrt(dom * b...  53.4 us
    pallas_call x1, Pallas kernels, shards(): pl.pallas_call(build, grid=(blk,), out_shape=(jax.ShapeDtypeStruct((blk,...  6.54 us
    pallas_call x1, Pallas kernels, shards(): pl.pallas_call(deliver, out_shape=shapes, in_specs=[vmem] * 4, out_specs=...  2.08 us

profile of v3, /device:TPU:0, one launch (start us, length us, event | category | flops | bytes accessed | tf_op | source)
XLA Modules:
  0.0 62.7 jit_solution(2709011770866167309)
XLA Ops:
  0.6 6.5 %shard_map.138 = (bf16[4,1024,1024]{2,1,0:T(8,128)(2,1)}, bf16[1024,384]{1,0:T(8,128)(2,1)}, bf16[8,48,128]{2,1,0:T(8,128)(2,1)}) custom-call(s32[1,4]{1,0:T(1,128)} %counts.1, s32[1,72]{1,0:T(1,128)} %rows.1, s32[1,72]{1,0:T(1,128)} %cols.1, s32[1,8]{1,0:T(1,128)} %send_counts.1, bf16[72,128,128]{2,1,0:T(8,128)(2,1)} %tiles.1, s32[1,384]{1,0:T(1,128)} %send_idx.1, ...), custom_call_target="tpu_custom_call" | custom-call | tf_op jit(solution)/shard_map/pallas_call | solution.py:291
  7.2 53.4 %shard_map.139 = (bf16[1024,256]{1,0:T(8,128)(2,1)}, bf16[1024,128]{1,0:T(8,128)(2,1)}, f32[128,256]{1,0:T(8,128)}, f32[1,256]{1,0:T(1,128)}) custom-call(bf16[4,1024,1024]{2,1,0:T(8,128)(2,1)} %get-tuple-element.15.a_hbm, bf16[1024,128]{1,0:T(8,128)(2,1)} %x.3, bf16[1024,384]{1,0:T(8,128)(2,1)} %cut_hbm.1, bf16[1024,384]{1,0:T(8,128)(2,1)} %get-tuple-element.16.picks_hbm, ...), custom_call_target="tpu_custom_call" | custom-call | tf_op jit(solution)/shard_map/pallas_call | solution.py:318
  60.6 2.1 %shard_map.140 = (bf16[1024,256]{1,0:T(8,128)(2,1)}, bf16[1024,128]{1,0:T(8,128)(2,1)}, f32[128,256]{1,0:T(8,128)}, f32[1,256]{1,0:T(1,128)}) custom-call(bf16[1024,256]{1,0:T(8,128)(2,1)} %get-tuple-element.18.refs_0_, bf16[1024,128]{1,0:T(8,128)(2,1)} %get-tuple-element.19.refs_1_, f32[128,256]{1,0:T(8,128)} %get-tuple-element.20.refs_2_, ...), custom_call_target="tpu_custom_call" | custom-call | tf_op jit(solution)/shard_map/pallas_call | solution.py:351
